TPU v7x, 32 devices: a whole 2x2x4 slice. The times are simulated.
32 devices in a mesh: tensor: 4 (over x, core), request: 8 (over z, y).
Axes of the slice: x: 2, y: 2, z: 4, core: 2. Of those that a mesh axis runs over, the one named last changes fastest.
Arguments:
- hidden_in: bfloat16 [2048, 2048], P('request'), may hold values from -6 to 6
- span_q: bfloat16 [2048, 2048], P('request', 'tensor'), may hold values from -170 to 170
- span_k: bfloat16 [2048, 2048], P('request', 'tensor'), may hold values from -7 to 7
- span_v: bfloat16 [2048, 2048], P('request', 'tensor'), may hold values from -6 to 6
- cache_k: bfloat16 [8, 768, 2048], P('request', None, 'tensor'), may hold values from -6 to 6
- cache_v: bfloat16 [8, 768, 2048], P('request', None, 'tensor'), may hold values from -6 to 6
- cached_len: int32 [8], P('request'), may hold values from 0 to 768
- out_proj: bfloat16 [2048, 2048], P('tensor'), may hold values from -0.125 to 0.125
- norm_gain: float32 [2048], replicated, may hold values from 0.1 to 1.9
- routes: int32 [2048, 4], P('request'), may hold values from 0 to 7, all different within a row; in each aligned block of 256 rows (0 to 255, 256 to 511, ...) at most 256 rows name the same one
- route_weight: float32 [2048, 4], P('request'), may hold values from 0.1 to 1
- w_gate: bfloat16 [8, 2048, 1408], P('request', None, 'tensor'), may hold values from -0.125 to 0.125
- w_up: bfloat16 [8, 2048, 1408], P('request', None, 'tensor'), may hold values from -0.125 to 0.125
- w_down: bfloat16 [8, 1408, 2048], P('request', 'tensor'), may hold values from -0.15625 to 0.15625
Outputs:
- layer_out: bfloat16 [2048, 2048], P('request', 'tensor')
- decode_kv: bfloat16 [8, 2, 1024, 2048], P('request', None, 'tensor')
Inputs may be any that keep to these rules, and one draw needn't show every extreme that they name: `routes`: among the rows of one request no expert is named more than 256 times.
All inputs are finite; a program needn't handle non-finite values.
Results may differ from a plain program's by a relative error of at most 0.014.
Values may be sent and summed in bfloat16 or wider, within the bound.
A program may use at most 128 MiB of HBM per device.

v0:
```python
import jax
import jax.numpy as jnp
from jax import lax
from jax.sharding import PartitionSpec as P

HD = 128
TOP = 4


eps = 1e-06
neg_large = -1e30


def attend(span_q, span_k, span_v, cache_k, cache_v, length):
    span = span_q.shape[0]
    prior = cache_k.shape[1]
    heads = span_q.shape[1] // HD
    keys = jnp.concatenate([cache_k[0], span_k], axis=0).reshape(prior + span, heads, HD)
    values = jnp.concatenate([cache_v[0], span_v], axis=0).reshape(prior + span, heads, HD)
    query = span_q.reshape(span, heads, HD)
    scores = jnp.einsum("qhd,khd->hqk", query, keys, preferred_element_type=jnp.float32) * HD ** (
        -0.5
    )
    key_pos = jnp.arange(prior + span, dtype=jnp.int32)[None, :]
    row_pos = jnp.arange(span, dtype=jnp.int32)[:, None]
    valid = jnp.where(key_pos < prior, key_pos < length, key_pos - prior <= row_pos)
    scores = jnp.where(valid[None], scores, neg_large)
    top = jnp.max(scores, axis=2, keepdims=True)
    weights = jnp.exp(scores - top)
    probs = (weights / jnp.sum(weights, axis=2, keepdims=True)).astype(jnp.bfloat16)
    attended = jnp.einsum("hqk,khd->qhd", probs, values, preferred_element_type=jnp.float32)
    return attended.astype(jnp.bfloat16).reshape(span, heads * HD)


def place(cached, fresh, length, context):
    span = fresh.shape[0]
    positions = jnp.arange(context, dtype=jnp.int32)
    padded = jnp.concatenate([cached[0], jnp.zeros((span, cached.shape[2]), cached.dtype)], axis=0)
    kept = jnp.where((positions < length)[:, None], padded, jnp.zeros_like(padded))
    return lax.dynamic_update_slice(kept, fresh, (length, jnp.int32(0)))


def on_device(
    hidden_in,
    span_q,
    span_k,
    span_v,
    cache_k,
    cache_v,
    cached_len,
    out_proj,
    norm_gain,
    routes,
    route_weight,
    w_gate,
    w_up,
    w_down,
):
    span, width = hidden_in.shape
    groups = lax.axis_size("tensor")
    quarter = width // groups
    offset = lax.axis_index("tensor") * quarter
    length = cached_len[0]
    attended = attend(span_q, span_k, span_v, cache_k, cache_v, length)
    attn_part = jnp.dot(attended, out_proj, preferred_element_type=jnp.float32)
    attn_full = lax.psum(attn_part.astype(jnp.bfloat16), "tensor").astype(jnp.float32)
    mixed = (hidden_in.astype(jnp.float32) + attn_full).astype(jnp.bfloat16)
    mixed_f = mixed.astype(jnp.float32)
    normed = (
        mixed_f * lax.rsqrt(jnp.mean(mixed_f * mixed_f, axis=1, keepdims=True) + eps) * norm_gain
    ).astype(jnp.bfloat16)
    own_mixed = lax.dynamic_slice_in_dim(mixed, offset, quarter, 1)
    experts = lax.axis_size("request")
    most = max(2, 2 * span * TOP // experts)
    flat = routes.reshape(-1)
    onehot = (flat[:, None] == jnp.arange(experts, dtype=jnp.int32)[None, :]).astype(jnp.int32)
    before = jnp.cumsum(onehot, axis=0) - onehot
    slot = jnp.sum(before * onehot, axis=1)
    dest = flat * most + slot
    source_row = jnp.arange(span * TOP, dtype=jnp.int32) // TOP
    outbox = (
        jnp.zeros((experts * most, normed.shape[1]), jnp.bfloat16).at[dest].set(normed[source_row])
    )
    inbox = lax.all_to_all(outbox, "request", split_axis=0, concat_axis=0, tiled=True)
    gate_w = w_gate[0]
    up_w = w_up[0]
    down_w = w_down[0]
    gate = jnp.dot(inbox, gate_w, preferred_element_type=jnp.float32)
    upper = jnp.dot(inbox, up_w, preferred_element_type=jnp.float32)
    act = (jax.nn.silu(gate) * upper).astype(jnp.bfloat16)
    partial_out = jnp.dot(act, down_w, preferred_element_type=jnp.float32)
    shares = lax.psum_scatter(
        partial_out.astype(jnp.bfloat16), "tensor", scatter_dimension=1, tiled=True
    )
    returned = lax.all_to_all(shares, "request", split_axis=0, concat_axis=0, tiled=True)
    picked = returned[dest].reshape(span, TOP, quarter).astype(jnp.float32)
    mixture = jnp.sum(picked * route_weight[:, :, None], axis=1)
    layer_out = (own_mixed.astype(jnp.float32) + mixture).astype(jnp.bfloat16)
    context = cache_k.shape[1] + span
    local = jnp.stack(
        [place(cache_k, span_k, length, context), place(cache_v, span_v, length, context)], axis=0
    )[None]
    decode_kv = lax.all_to_all(local, "tensor", split_axis=2, concat_axis=3, tiled=True)
    return (layer_out, decode_kv)


def solution(mesh):
    in_specs = (
        P("request", None),
        P("request", "tensor"),
        P("request", "tensor"),
        P("request", "tensor"),
        P("request", None, "tensor"),
        P("request", None, "tensor"),
        P("request"),
        P("tensor", None),
        P(),
        P("request", None),
        P("request", None),
        P("request", None, "tensor"),
        P("request", None, "tensor"),
        P("request", "tensor", None),
    )
    out_specs = (P("request", "tensor"), P("request", None, "tensor", None))
    return jax.shard_map(
        on_device, mesh=mesh, in_specs=in_specs, out_specs=out_specs, check_vma=False
    )
```

profile of v0, /device:TPU:0, one launch (start us, length us, event | category | flops | bytes accessed | tf_op | source)
XLA Modules:
  0.0 453.4 jit_solution(6738885702415834086)
XLA Ops:
  11.5 1.8 copy.54
  13.3 2.3 copy.49
  19.1 2.1 fusion.36
  24.0 2.3 reduce-window.6
  27.2 35.4 %all-reduce.4.cloned.1.call-done = bf16[256,2048]{1,0:T(8,128)(2,1)} async-done(((bf16[256,2048]{1,0:T(8,128)(2,1)}), bf16[256,2048]{1,0:T(8,128)(2,1)}) %all-reduce.4.cloned.1.call-update) | async-done | bytes 1048592 | tf_op jit(solution)/shard_map/psum | solution.py:66
  62.5 2.0 fusion.6
  64.9 25.1 %scatter_custom_fusion = bf16[2048,2048]{1,0:T(8,128)(2,1)} fusion(s32[1024]{0:T(1024)S(1)} %bitcast.98, bf16[256,2048]{1,0:T(8,128)(2,1)S(1)} %fusion.8, s32[1024]{0:T(1024)S(1)} %broadcast_clamp_fusion.1, bf16[]{:T(256)} %constant.54.clone.1), kind=kCustom, calls=%fused_computation.6 | custom fusion | bytes 8388610 | tf_op jit(solution)/shard_map/scatter | solution.py:82
  90.0 188.7 %all_to_all.42 = bf16[8,256,2048]{2,1,0:T(8,128)(2,1)S(1)} all-to-all(bf16[8,256,2048]{2,1,0:T(8,128)(2,1)} %bitcast.83), channel_id=1, replica_groups=mesh['tensor'=4,'request'=8] {'request'}, dimensions={0} | all-to-all | bytes 16777216 | tf_op jit(solution)/shard_map/all_to_all | solution.py:84
  278.7 3.2 fusion.15
  282.0 3.5 fusion.5
  285.5 6.9 %convolution_convert_fusion = bf16[2048,2048]{1,0:T(8,128)(2,1)} fusion(bf16[2048,352]{0,1:T(8,128)(2,1)S(1)} %fusion.5, bf16[1,352,2048]{2,1,0:T(8,128)(2,1)S(1)} %copy-done.15), kind=kOutput, calls=%fused_computation.4 | convolution fusion | flops 2956984320 | bytes 11272192 | tf_op jit(solution)/shard_map/dot_general | solution.py:91
  293.5 2.5 select_bitcast_fusion.1
  298.4 1.9 dynamic_update_slice.9
  300.3 2.3 maximum_bitcast_fusion
  302.5 2.2 copy.61
  304.7 45.1 %all_to_all.43 = bf16[1,2,1024,512]{3,1,0,2:T(2,128)(2,1)S(1)} all-to-all(bf16[1,2,1024,512]{3,1,0,2:T(2,128)(2,1)S(1)} %copy.61), channel_id=1, replica_groups=mesh['tensor'=4,'request'=8] {'tensor'}, dimensions={2} | all-to-all | bytes 4194304 | tf_op jit(solution)/shard_map/all_to_all | solution.py:103
  349.8 29.4 %reduce-scatter.2.cloned.1.call-done = bf16[2048,512]{1,0:T(8,128)(2,1)} async-done(((bf16[2048,2048]{1,0:T(8,128)(2,1)}), bf16[2048,512]{1,0:T(8,128)(2,1)}) %reduce-scatter.2.cloned.1.call-update) | async-done | bytes 2097168 | tf_op jit(solution)/shard_map/reduce_scatter | solution.py:92
  379.2 4.7 %all-to-all-start.1 = ((bf16[8,256,512]{2,1,0:T(8,128)(2,1)}), bf16[8,256,512]{2,1,0:T(8,128)(2,1)}, u32[]{:S(2)}, u32[]{:S(2)}) async-start(bf16[8,256,512]{2,1,0:T(8,128)(2,1)} %bitcast.90), calls=%async_computation.2 | async-start | bytes 4194304 | tf_op jit(solution)/shard_map/all_to_all | solution.py:95
  384.1 2.9 copy.62
  387.1 4.4 all_to_all.38
  391.5 41.0 %all-to-all-done.1 = bf16[8,256,512]{2,1,0:T(8,128)(2,1)} async-done(((bf16[8,256,512]{2,1,0:T(8,128)(2,1)}), bf16[8,256,512]{2,1,0:T(8,128)(2,1)}, u32[]{:S(2)}, u32[]{:S(2)}) %all-to-all-start.1) | async-done | bytes 2097184 | tf_op jit(solution)/shard_map/all_to_all | solution.py:95
  432.5 7.1 %gather_fusion = bf16[1024,512]{1,0:T(8,128)(2,1)} fusion(bf16[2048,512]{1,0:T(8,128)(2,1)} %bitcast.18, s32[1024]{0:T(1024)S(1)} %broadcast_clamp_fusion), kind=kCustom, calls=%fused_computation.1 | custom fusion | bytes 2101248 | tf_op jit(solution)/shard_map/gather | solution.py:96
  439.6 2.8 reshape.201
  442.4 2.9 multiply_reduce_fusion
  (66 shorter events, 15.2 us)
Async XLA Ops:
  7.2 14.6 %copy-start = (bf16[512,2048]{1,0:T(8,128)(2,1)S(1)}, bf16[512,2048]{1,0:T(8,128)(2,1)}, u32[]{:S(2)}) copy-start(bf16[512,2048]{1,0:T(8,128)(2,1)} %param.21) | copy-start | bytes 6291460
  7.2 3.5 copy-start.5
  7.2 55.3 %all-reduce.4.cloned.1.call-start = ((), (), s32[]{:S(2)}) async-start(), calls=%async_computation.4 | async-start | bytes 2097152 | tf_op jit(solution)/shard_map/psum | solution.py:66
  8.1 7.6 %copy-start.6 = (bf16[256,512]{1,0:T(8,128)(2,1)S(1)}, bf16[256,512]{1,0:T(8,128)(2,1)}, u32[]{:S(2)}) copy-start(bf16[256,512]{1,0:T(8,128)(2,1)} %param.17) | copy-start | bytes 786436
  10.7 6.6 %copy-start.4 = (bf16[768,4,128]{2,0,1:T(8,128)(2,1)S(1)}, bf16[768,4,128]{2,0,1:T(8,128)(2,1)}, u32[]{:S(2)}) copy-start(bf16[768,4,128]{2,0,1:T(8,128)(2,1)} %copy.53) | copy-start | bytes 2359300
  19.1 2.2 copy-start.8
  19.1 2.2 copy-start.9
  21.8 1.8 copy-start.10
  23.5 41.1 %copy-start.11 = (f32[2048]{0:T(1024)S(1)}, f32[2048]{0:T(1024)}, u32[]{:S(2)}) copy-start(f32[2048]{0:T(1024)} %param.22) | copy-start | bytes 24580
  23.5 355.7 %reduce-scatter.2.cloned.1.call-start = ((), (), s32[]{:S(2)}) async-start(), calls=%async_computation.5 | async-start | bytes 10485760 | tf_op jit(solution)/shard_map/reduce_scatter | solution.py:92
  90.0 188.7 %copy-start.13 = (bf16[1,2048,352]{1,2,0:T(8,128)(2,1)S(1)}, bf16[1,2048,352]{1,2,0:T(8,128)(2,1)}, u32[]{:S(2)}) copy-start(bf16[1,2048,352]{1,2,0:T(8,128)(2,1)} %param.25) | copy-start | bytes 4325380
  278.7 3.2 copy-start.14
  282.0 3.5 copy-start.15
  292.4 1.1 copy-start.3
  292.4 6.0 %copy-start.7 = (bf16[256,512]{1,0:T(8,128)(2,1)S(1)}, bf16[256,512]{1,0:T(8,128)(2,1)}, u32[]{:S(2)}) copy-start(bf16[256,512]{1,0:T(8,128)(2,1)} %param.17) | copy-start | bytes 786436
  297.4 1.0 copy-start.2
  349.8 34.2 %copy-start.12 = (f32[256,4]{0,1:T(4,128)S(1)}, f32[256,4]{0,1:T(4,128)}, u32[]{:S(2)}) copy-start(f32[256,4]{0,1:T(4,128)} %param.24) | copy-start | bytes 12292
  379.2 53.3 %all-to-all-start.1 = ((bf16[8,256,512]{2,1,0:T(8,128)(2,1)}), bf16[8,256,512]{2,1,0:T(8,128)(2,1)}, u32[]{:S(2)}, u32[]{:S(2)}) async-start(bf16[8,256,512]{2,1,0:T(8,128)(2,1)} %bitcast.90), calls=%async_computation.2 | async-start | bytes 4194304 | tf_op jit(solution)/shard_map/all_to_all | solution.py:95
  432.5 13.6 %copy-start.1 = (bf16[512,2048]{1,0:T(8,128)(2,1)S(1)}, bf16[512,2048]{1,0:T(8,128)(2,1)}, u32[]{:S(2)}) copy-start(bf16[512,2048]{1,0:T(8,128)(2,1)} %param.21) | copy-start | bytes 6291460
Sparse Core Ops, SparseCore 0:
  23.7 38.8 all-reduce.3
  292.5 86.6 reduce-scatter.1
where the time goes:
time: 460 us; the launch traced here: 453 us
  blocking collectives  234 us (51%)
  waiting for transfers between devices  106 us (23%)
  local copies, waits for them, and re-layouts  59.3 us (13%)
  matrix products  17.6 us (4%)
  other arithmetic  16.4 us (4%)
  between operations  15.7 us (3%)
  starting transfers between devices  4.83 us (1%)
    all_to_all x1, blocking collectives, on_device(): lax.all_to_all(outbox, 'request', split_axis=0, concat_axis=0, tiled=True)  189 us
    all_to_all x1, blocking collectives, on_device(): lax.all_to_all(local, 'tensor', split_axis=2, concat_axis=3, tiled=True)  45.1 us
    all_to_all x1, waiting for transfers between devices, on_device(): lax.all_to_all(shares, 'request', split_axis=0, concat_axis=0, tiled=True)  41 us
    psum x1, waiting for transfers between devices, on_device(): lax.psum(attn_part.astype(jnp.bfloat16), 'tensor').astype(jnp.float32)  35.4 us
    reduce_scatter x1, waiting for transfers between devices, on_device(): lax.psum_scatter(partial_out.astype(jnp.bfloat16), 'tensor', scatter_dime...  29.4 us
    scatter x1, local copies, waits for them, and re-layouts, on_device(): jnp.zeros((experts * most, normed.shape[1]), jnp.bfloat16).at[dest]  25.1 us
  transfers between devices with their start and end apart: 3, of which 3 were waited for; matrix products, arithmetic and copies ran while one was open for 4% of the time, Pallas kernels for 0%

commit v1 on v0

--- a/solution.py
+++ b/solution.py
@@ -40,6 +40,50 @@
     return lax.dynamic_update_slice(kept, fresh, (length, jnp.int32(0)))
 
 
+def all_tokens(normed, routes, route_weight, gate_w, up_w, down_w, experts):
+    ids = jnp.arange(experts, dtype=jnp.int32)
+    spread = jnp.sum(
+        jnp.where(routes[:, :, None] == ids, route_weight[:, :, None], 0.0), axis=1
+    )
+    weights = lax.all_to_all(spread, "request", split_axis=1, concat_axis=0, tiled=True)
+    tokens = lax.all_gather(normed, "request", axis=0, tiled=True)
+    gate = jnp.dot(tokens, gate_w, preferred_element_type=jnp.float32)
+    upper = jnp.dot(tokens, up_w, preferred_element_type=jnp.float32)
+    act = (jax.nn.silu(gate) * upper * weights).astype(jnp.bfloat16)
+    part = jnp.dot(act, down_w, preferred_element_type=jnp.float32).astype(jnp.bfloat16)
+    shares = lax.psum_scatter(part, "tensor", scatter_dimension=1, tiled=True)
+    total = lax.psum_scatter(shares, "request", scatter_dimension=0, tiled=True)
+    return total.astype(jnp.float32)
+
+
+def by_slots(normed, routes, route_weight, gate_w, up_w, down_w, experts, most):
+    span = normed.shape[0]
+    flat = routes.reshape(-1)
+    onehot = (flat[:, None] == jnp.arange(experts, dtype=jnp.int32)[None, :]).astype(jnp.float32)
+    rows = jnp.arange(span * TOP, dtype=jnp.int32)
+    earlier = (rows[None, :] < rows[:, None]).astype(jnp.bfloat16)
+    before = jnp.dot(earlier, onehot.astype(jnp.bfloat16), preferred_element_type=jnp.float32)
+    slot = jnp.sum(before * onehot, axis=1).astype(jnp.int32)
+    dest = (flat * most + slot).reshape(span, TOP)
+    slots = jnp.arange(experts * most, dtype=jnp.int32)
+    hit = dest[:, :, None] == slots
+    send = jnp.any(hit, axis=1).astype(jnp.bfloat16)
+    outbox = lax.dot_general(
+        send, normed, (((0,), (0,)), ((), ())), preferred_element_type=jnp.float32
+    ).astype(jnp.bfloat16)
+    inbox = lax.all_to_all(outbox, "request", split_axis=0, concat_axis=0, tiled=True)
+    gate = jnp.dot(inbox, gate_w, preferred_element_type=jnp.float32)
+    upper = jnp.dot(inbox, up_w, preferred_element_type=jnp.float32)
+    act = (jax.nn.silu(gate) * upper).astype(jnp.bfloat16)
+    partial_out = jnp.dot(act, down_w, preferred_element_type=jnp.float32)
+    shares = lax.psum_scatter(
+        partial_out.astype(jnp.bfloat16), "tensor", scatter_dimension=1, tiled=True
+    )
+    returned = lax.all_to_all(shares, "request", split_axis=0, concat_axis=0, tiled=True)
+    weigh = jnp.sum(jnp.where(hit, route_weight[:, :, None], 0.0), axis=1)
+    return jnp.dot(weigh, returned.astype(jnp.float32), precision=lax.Precision.HIGHEST)
+
+
 def on_device(
     hidden_in,
     span_q,
@@ -72,29 +116,12 @@
     own_mixed = lax.dynamic_slice_in_dim(mixed, offset, quarter, 1)
     experts = lax.axis_size("request")
     most = max(2, 2 * span * TOP // experts)
-    flat = routes.reshape(-1)
-    onehot = (flat[:, None] == jnp.arange(experts, dtype=jnp.int32)[None, :]).astype(jnp.int32)
-    before = jnp.cumsum(onehot, axis=0) - onehot
-    slot = jnp.sum(before * onehot, axis=1)
-    dest = flat * most + slot
-    source_row = jnp.arange(span * TOP, dtype=jnp.int32) // TOP
-    outbox = (
-        jnp.zeros((experts * most, normed.shape[1]), jnp.bfloat16).at[dest].set(normed[source_row])
-    )
-    inbox = lax.all_to_all(outbox, "request", split_axis=0, concat_axis=0, tiled=True)
-    gate_w = w_gate[0]
-    up_w = w_up[0]
-    down_w = w_down[0]
-    gate = jnp.dot(inbox, gate_w, preferred_element_type=jnp.float32)
-    upper = jnp.dot(inbox, up_w, preferred_element_type=jnp.float32)
-    act = (jax.nn.silu(gate) * upper).astype(jnp.bfloat16)
-    partial_out = jnp.dot(act, down_w, preferred_element_type=jnp.float32)
-    shares = lax.psum_scatter(
-        partial_out.astype(jnp.bfloat16), "tensor", scatter_dimension=1, tiled=True
-    )
-    returned = lax.all_to_all(shares, "request", split_axis=0, concat_axis=0, tiled=True)
-    picked = returned[dest].reshape(span, TOP, quarter).astype(jnp.float32)
-    mixture = jnp.sum(picked * route_weight[:, :, None], axis=1)
+    if most >= span:
+        mixture = all_tokens(normed, routes, route_weight, w_gate[0], w_up[0], w_down[0], experts)
+    else:
+        mixture = by_slots(
+            normed, routes, route_weight, w_gate[0], w_up[0], w_down[0], experts, most
+        )
     layer_out = (own_mixed.astype(jnp.float32) + mixture).astype(jnp.bfloat16)
     context = cache_k.shape[1] + span
     local = jnp.stack(

time: 460 us -> 365 us (0.79); the launches traced: 453 us -> 365 us
  blocking collectives: 234 us -> 0 us
  waiting for transfers between devices: 106 us -> 272 us
  local copies, waits for them, and re-layouts: 59.3 us -> 27.1 us
  matrix products: 17.6 us -> 27.6 us
  starting transfers between devices: 4.83 us -> 10.3 us
    all_to_all x2 -> x0, blocking collectives: 234 us -> none  [the longest x1 189 us: on_device(): lax.all_to_all(outbox, 'request', split_axis=0, concat_axis=0, tiled=True)]
    all_gather x0 -> x1, waiting for transfers between devices: none -> 119 us  [all_tokens(): tokens = lax.all_gather(normed, 'request', axis=0, tiled=True)]
    reduce_scatter x1 -> x2, waiting for transfers between devices: 29.4 us -> 88.2 us  [the longest x1 70 us: all_tokens(): shares = lax.psum_scatter(part, 'tensor', scatter_dimension=1, tiled=True)]
    scatter x1 -> x0, local copies, waits for them, and re-layouts: 25.1 us -> none  [on_device(): jnp.zeros((experts * most, normed.shape[1]), jnp.bfloat16).at[dest]]
    all_to_all x1 -> x2, waiting for transfers between devices: 41 us -> 25.8 us  [the longest x1 25.8 us: on_device(): lax.all_to_all(local, 'tensor', split_axis=2, concat_axis=3, tiled=True)]
    dot_general x3, matrix products: 13.6 us -> 23.6 us  [the longest x1 8.57 us: all_tokens(): gate = jnp.dot(tokens, gate_w, preferred_element_type=jnp.float32)]
    gather x1 -> x0, local copies, waits for them, and re-layouts: 7.12 us -> none  [on_device(): picked = returned[dest].reshape(span, TOP, quarter).astype(jnp.float32)]
    all_to_all x1 -> x2, starting transfers between devices: 4.75 us -> 9.97 us  [the longest x1 5.52 us: all_tokens(): lax.all_to_all(spread, 'request', split_axis=1, concat_axis=0, tiled=True)]
  transfers between devices with their start and end apart: 3 -> 6, of which waited for: 3 -> 5; matrix products, arithmetic and copies ran while one was open for 4% -> 8% of each run, Pallas kernels for 0% -> 0%
where the time goes in v1:
time: 365 us
  waiting for transfers between devices  272 us (75%)
  matrix products  27.6 us (8%)
  local copies, waits for them, and re-layouts  27.1 us (7%)
  between operations  14.8 us (4%)
  other arithmetic  12.8 us (4%)
  starting transfers between devices  10.3 us (3%)
    all_gather x1, waiting for transfers between devices, all_tokens(): tokens = lax.all_gather(normed, 'request', axis=0, tiled=True)  119 us
    reduce_scatter x1, waiting for transfers between devices, all_tokens(): shares = lax.psum_scatter(part, 'tensor', scatter_dimension=1, tiled=True)  70 us
    psum x1, waiting for transfers between devices, on_device(): lax.psum(attn_part.astype(jnp.bfloat16), 'tensor').astype(jnp.float32)  38.9 us
    all_to_all x1, waiting for transfers between devices, on_device(): lax.all_to_all(local, 'tensor', split_axis=2, concat_axis=3, tiled=True)  25.8 us
    reduce_scatter x1, waiting for transfers between devices, all_tokens(): total = lax.psum_scatter(shares, 'request', scatter_dimension=0, tiled=True)  18.2 us
    all_to_all x2, local copies, waits for them, and re-layouts, on_device(): lax.all_to_all(local, 'tensor', split_axis=2, concat_axis=3, tiled=True)  9 us
    dot_general x1, matrix products, all_tokens(): gate = jnp.dot(tokens, gate_w, preferred_element_type=jnp.float32)  8.57 us
    dot_general x1, matrix products, all_tokens(): upper = jnp.dot(tokens, up_w, preferred_element_type=jnp.float32)  8.13 us
  transfers between devices with their start and end apart: 6, of which 5 were waited for; matrix products, arithmetic and copies ran while one was open for 8% of the time, Pallas kernels for 0%

profile of v1, /device:TPU:0, one launch (start us, length us, event | category | flops | bytes accessed | tf_op | source)
XLA Modules:
  0.0 364.6 jit_solution(15921844279259486058)
XLA Ops:
  11.5 1.8 copy.63
  13.3 2.3 copy.58
  17.3 1.7 fusion.19
  19.0 2.1 fusion.30
  21.7 1.7 convolution_convert_fusion.1
  23.5 38.9 %all-reduce.4.cloned.1.call-done = bf16[256,2048]{1,0:T(8,128)(2,1)} async-done(((bf16[256,2048]{1,0:T(8,128)(2,1)}), bf16[256,2048]{1,0:T(8,128)(2,1)}) %all-reduce.4.cloned.1.call-update) | async-done | bytes 1048592 | tf_op jit(solution)/shard_map/psum | solution.py:110
  62.4 2.0 fusion.4
  66.5 5.5 %all-to-all-start = ((f32[256,8,1]{0,2,1:T(1,128)}), f32[256,8,1]{0,2,1:T(1,128)S(1)}, u32[]{:S(2)}, u32[]{:S(2)}) async-start(f32[256,8,1]{0,2,1:T(1,128)} %copy.66), calls=%async_computation | async-start | bytes 16384 | tf_op jit(solution)/shard_map/all_to_all | solution.py:48
  72.2 119.1 %all-gather.2.cloned.1.call-done = bf16[2048,2048]{1,0:T(8,128)(2,1)} async-done(((bf16[256,2048]{1,0:T(8,128)(2,1)}), bf16[2048,2048]{1,0:T(8,128)(2,1)}) %all-gather.2.cloned.1.call-update) | async-done | bytes 8388624 | tf_op jit(solution)/shard_map/all_gather | solution.py:49
  191.3 8.6 %fusion.13 = f32[2048,352]{0,1:T(8,128)} fusion(bf16[2048,2048]{1,0:T(8,128)(2,1)} %all-gather.2.cloned.1.call-done, bf16[1,2048,352]{1,2,0:T(8,128)(2,1)} %param.25), kind=kOutput, calls=%fused_computation.23 | convolution fusion | flops 2952790016 | bytes 12713984 | tf_op jit(solution)/shard_map/dot_general | solution.py:50
  199.9 8.1 %fusion.3 = bf16[2048,352]{0,1:T(8,128)(2,1)S(1)} fusion(bf16[2048,2048]{1,0:T(8,128)(2,1)} %all-gather.2.cloned.1.call-done, f32[2048,352]{0,1:T(8,128)} %fusion.13, bf16[1,2048,352]{1,2,0:T(8,128)(2,1)} %param.26, f32[2048]{0:T(1024)S(1)} %bitcast.71), kind=kOutput, calls=%fused_computation.8 | convolution fusion | flops 2957836288 | bytes 14163968 | tf_op jit(solution)/shard_map/dot_general | solution.py:51
  208.0 6.9 %convolution_convert_fusion = bf16[2048,2048]{1,0:T(8,128)(2,1)} fusion(bf16[2048,352]{0,1:T(8,128)(2,1)S(1)} %fusion.3, bf16[1,352,2048]{2,1,0:T(8,128)(2,1)S(1)} %copy-done.9), kind=kOutput, calls=%fused_computation.1 | convolution fusion | flops 2956984320 | bytes 11272192 | tf_op jit(solution)/shard_map/dot_general | solution.py:53
  215.0 70.0 %reduce-scatter.3.cloned.1.call-done = bf16[2048,512]{1,0:T(8,128)(2,1)} async-done(((bf16[2048,2048]{1,0:T(8,128)(2,1)}), bf16[2048,512]{1,0:T(8,128)(2,1)}) %reduce-scatter.3.cloned.1.call-update) | async-done | bytes 2097168 | tf_op jit(solution)/shard_map/reduce_scatter | solution.py:54
  285.0 3.0 select_bitcast_fusion.1
  288.1 2.8 dynamic_update_slice.8
  290.9 2.8 dynamic_update_slice.9
  293.7 1.7 maximum_bitcast_fusion
  295.4 3.5 copy.67
  298.9 4.5 %all-to-all-start.1 = ((bf16[1,2,1024,512]{3,1,0,2:T(2,128)(2,1)}), bf16[1,2,1024,512]{3,1,0,2:T(2,128)(2,1)}, u32[]{:S(2)}, u32[]{:S(2)}) async-start(bf16[1,2,1024,512]{3,1,0,2:T(2,128)(2,1)} %copy.67), calls=%async_computation.3 | async-start | bytes 4194304 | tf_op jit(solution)/shard_map/all_to_all | solution.py:130
  303.4 25.8 %all-to-all-done.1 = bf16[1,2,1024,512]{3,1,0,2:T(2,128)(2,1)} async-done(((bf16[1,2,1024,512]{3,1,0,2:T(2,128)(2,1)}), bf16[1,2,1024,512]{3,1,0,2:T(2,128)(2,1)}, u32[]{:S(2)}, u32[]{:S(2)}) %all-to-all-start.1) | async-done | bytes 2097184 | tf_op jit(solution)/shard_map/all_to_all | solution.py:130
  329.1 4.6 %copy.68 = bf16[1,2,256,4,512]{4,3,2,1,0:T(4,128)(2,1)} copy(bf16[1,2,256,4,512]{4,1,2,3,0:T(2,128)(2,1)} %bitcast.22) | data formatting | bytes 4194304 | tf_op jit(solution)/shard_map/all_to_all | solution.py:130
  333.7 4.4 %all_to_all.31 = bf16[1,2,256,2048]{3,2,1,0:T(8,128)(2,1)} reshape(bf16[1,2,256,4,512]{4,3,2,1,0:T(4,128)(2,1)} %copy.68) | data formatting | bytes 4194304 | tf_op jit(solution)/shard_map/all_to_all | solution.py:130
  338.1 18.2 %reduce-scatter.5.cloned.1.call-done = bf16[256,512]{1,0:T(8,128)(2,1)} async-done(((bf16[2048,512]{1,0:T(8,128)(2,1)}), bf16[256,512]{1,0:T(8,128)(2,1)}) %reduce-scatter.5.cloned.1.call-update) | async-done | bytes 262160 | tf_op jit(solution)/shard_map/reduce_scatter | solution.py:55
  356.3 1.7 add_convert_fusion.1
  (41 shorter events, 8.0 us)
Async XLA Ops:
  7.2 14.6 %copy-start = (bf16[512,2048]{1,0:T(8,128)(2,1)S(1)}, bf16[512,2048]{1,0:T(8,128)(2,1)}, u32[]{:S(2)}) copy-start(bf16[512,2048]{1,0:T(8,128)(2,1)} %param.21) | copy-start | bytes 6291460
  7.2 3.5 copy-start.2
  7.2 55.3 %all-reduce.4.cloned.1.call-start = ((), (), s32[]{:S(2)}) async-start(), calls=%async_computation.4 | async-start | bytes 2097152 | tf_op jit(solution)/shard_map/psum | solution.py:110
  9.5 6.1 %copy-start.3 = (bf16[256,512]{1,0:T(8,128)(2,1)S(1)}, bf16[256,512]{1,0:T(8,128)(2,1)}, u32[]{:S(2)}) copy-start(bf16[256,512]{1,0:T(8,128)(2,1)} %param.17) | copy-start | bytes 786436
  10.7 6.6 %copy-start.1 = (bf16[768,4,128]{2,0,1:T(8,128)(2,1)S(1)}, bf16[768,4,128]{2,0,1:T(8,128)(2,1)}, u32[]{:S(2)}) copy-start(bf16[768,4,128]{2,0,1:T(8,128)(2,1)} %copy.62) | copy-start | bytes 2359300
  19.0 2.2 copy-start.4
  19.0 2.2 copy-start.5
  23.5 41.1 %copy-start.6 = (f32[2048]{0:T(1024)S(1)}, f32[2048]{0:T(1024)}, u32[]{:S(2)}) copy-start(f32[2048]{0:T(1024)} %param.22) | copy-start | bytes 24580
  23.5 167.8 %all-gather.2.cloned.1.call-start = ((), (), s32[]{:S(2)}) async-start(), calls=%async_computation.5 | async-start | bytes 9437184 | tf_op jit(solution)/shard_map/all_gather | solution.py:49
  64.5 1.4 copy-start.7
  64.5 1.3 copy-start.8
  66.5 133.4 %all-to-all-start = ((f32[256,8,1]{0,2,1:T(1,128)}), f32[256,8,1]{0,2,1:T(1,128)S(1)}, u32[]{:S(2)}, u32[]{:S(2)}) async-start(f32[256,8,1]{0,2,1:T(1,128)} %copy.66), calls=%async_computation | async-start | bytes 16384 | tf_op jit(solution)/shard_map/all_to_all | solution.py:48
  72.0 213.0 %reduce-scatter.3.cloned.1.call-start = ((), (), s32[]{:S(2)}) async-start(), calls=%async_computation.6 | async-start | bytes 10485760 | tf_op jit(solution)/shard_map/reduce_scatter | solution.py:54
  199.9 8.1 %copy-start.9 = (bf16[1,352,2048]{2,1,0:T(8,128)(2,1)S(1)}, bf16[1,352,2048]{2,1,0:T(8,128)(2,1)}, u32[]{:S(2)}) copy-start(bf16[1,352,2048]{2,1,0:T(8,128)(2,1)} %param.27) | copy-start | bytes 4325380
  214.9 141.4 %reduce-scatter.5.cloned.1.call-start = ((), (), s32[]{:S(2)}) async-start(), calls=%async_computation.7 | async-start | bytes 2359296 | tf_op jit(solution)/shard_map/reduce_scatter | solution.py:55
  298.9 30.2 %all-to-all-start.1 = ((bf16[1,2,1024,512]{3,1,0,2:T(2,128)(2,1)}), bf16[1,2,1024,512]{3,1,0,2:T(2,128)(2,1)}, u32[]{:S(2)}, u32[]{:S(2)}) async-start(bf16[1,2,1024,512]{3,1,0,2:T(2,128)(2,1)} %copy.67), calls=%async_computation.3 | async-start | bytes 4194304 | tf_op jit(solution)/shard_map/all_to_all | solution.py:130
Sparse Core Ops, SparseCore 0:
  23.6 38.7 all-reduce.3
  66.0 125.3 all-gather.1
  215.1 69.8 reduce-scatter.2
  288.4 67.9 reduce-scatter.4

commit v2 on v1

--- a/solution.py
+++ b/solution.py
@@ -1,6 +1,8 @@
 import jax
 import jax.numpy as jnp
 from jax import lax
+from jax.experimental import pallas as pl
+from jax.experimental.pallas import tpu as pltpu
 from jax.sharding import PartitionSpec as P
 
 HD = 128
@@ -40,20 +42,295 @@
     return lax.dynamic_update_slice(kept, fresh, (length, jnp.int32(0)))
 
 
-def all_tokens(normed, routes, route_weight, gate_w, up_w, down_w, experts):
+MESH = pl.DeviceIdType.MESH
+ROWS = 64
+
+
+def remote(src, dst, send, recv, device):
+    return pltpu.make_async_remote_copy(
+        src_ref=src,
+        dst_ref=dst,
+        send_sem=send,
+        recv_sem=recv,
+        device_id=device,
+        device_id_type=MESH,
+    )
+
+
+def position():
+    t, r = lax.axis_index("tensor"), lax.axis_index("request")
+    x, c, z, y = t // 2, t % 2, r // 2, r % 2
+    return t, r, x, c, z, y
+
+
+def meet(peers):
+    barrier = pltpu.get_barrier_semaphore()
+    for peer in peers:
+        pl.semaphore_signal(barrier, inc=1, device_id=peer, device_id_type=MESH)
+    pl.semaphore_wait(barrier, len(peers))
+
+
+def gather_kernel(
+    part, hidden, gain, local, tokens, mixed_out, decode,
+    recv_core, chip_sum, recv_x, mixed, normed,
+    m_send, m_recv, d_send, d_recv, z_send, z_recv, y_send, y_recv, s_send, s_recv, own_sem,
+):
+    t, r, x, c, z, y = position()
+    span, width = part.shape
+    half, quarter = width // 2, width // 4
+    depth = decode.shape[1]
+    sib = {"tensor": x * 2 + 1 - c}
+    across = {"tensor": (1 - x) * 2 + c}
+    corner = {"tensor": (1 - x) * 2 + 1 - c}
+    beside = {"request": z * 2 + 1 - y}
+    line = [{"request": ((z + d) % 4) * 2 + y} for d in (1, 2, 3)]
+    meet([sib, across, corner, beside] + line)
+    mine = pl.ds(pl.multiple_of(half * c, half), half)
+    other = pl.ds(pl.multiple_of(half * (1 - c), half), half)
+
+    core = remote(part.at[:, other], recv_core, m_send.at[0], m_recv.at[0], sib)
+    core.start()
+    core.wait_recv()
+
+    @pl.loop(0, span // ROWS)
+    def _(i):
+        rows = pl.ds(pl.multiple_of(i * ROWS, ROWS), ROWS)
+        total = part[rows, mine].astype(jnp.float32) + recv_core[rows, :].astype(jnp.float32)
+        chip_sum[rows, :] = total.astype(jnp.bfloat16)
+
+    cross = remote(chip_sum, recv_x, m_send.at[1], m_recv.at[1], across)
+    cross.start()
+    keep = pl.ds(pl.multiple_of(quarter * t, quarter), quarter)
+    moves = []
+    for j in (1, 2, 3):
+        peer = (t + j) % 4
+        there = pl.ds(pl.multiple_of(depth * peer, depth), depth)
+        moves.append(
+            remote(
+                local.at[:, there, :], decode.at[:, :, keep], d_send.at[j - 1], d_recv.at[j - 1],
+                {"tensor": peer},
+            )
+        )
+        moves[-1].start()
+    here = pl.ds(pl.multiple_of(depth * t, depth), depth)
+    stay = pltpu.make_async_copy(local.at[:, here, :], decode.at[:, :, keep], own_sem.at[0])
+    stay.start()
+    cross.wait_recv()
+
+    @pl.loop(0, span // ROWS)
+    def _(i):
+        rows = pl.ds(pl.multiple_of(i * ROWS, ROWS), ROWS)
+        total = chip_sum[rows, :].astype(jnp.float32) + recv_x[rows, :].astype(jnp.float32)
+        mixed[rows, mine] = (hidden[rows, mine].astype(jnp.float32) + total).astype(jnp.bfloat16)
+
+    share = remote(mixed.at[:, mine], mixed.at[:, mine], m_send.at[2], m_recv.at[2], sib)
+    share.start()
+    share.wait_recv()
+
+    @pl.loop(0, span // ROWS)
+    def _(i):
+        rows = pl.ds(pl.multiple_of(i * ROWS, ROWS), ROWS)
+        value = mixed[rows, :].astype(jnp.float32)
+        scale = lax.rsqrt(jnp.mean(value * value, axis=1, keepdims=True) + eps)
+        normed[rows, :] = (value * scale * gain[...]).astype(jnp.bfloat16)
+        mixed_out[rows, :] = mixed[rows, keep]
+
+    own = pltpu.make_async_copy(normed, tokens.at[r], own_sem.at[1])
+    own.start()
+    zs, ys, ss = [], [], []
+    for d in (2, 1, 3):
+        zs.append(
+            remote(
+                normed.at[:, mine], tokens.at[r, :, mine], z_send.at[d - 1], z_recv.at[d - 1],
+                line[d - 1],
+            )
+        )
+    ys.append(
+        remote(normed.at[:, mine], tokens.at[r, :, mine], y_send.at[0], y_recv.at[0], beside)
+    )
+    for copy in ys + zs:
+        copy.start()
+
+    def to_sib(k, block):
+        view = tokens.at[block, :, mine]
+        ss.append(remote(view, view, s_send.at[k], s_recv.at[k], sib))
+        ss[-1].start()
+
+    ys[0].wait_recv()
+    to_sib(0, z * 2 + 1 - y)
+    for k, d in enumerate((2, 1, 3)):
+        zs[k].wait_recv()
+        block = ((z + 4 - d) % 4) * 2 + y
+        view = tokens.at[block, :, mine]
+        ys.append(remote(view, view, y_send.at[k + 1], y_recv.at[k + 1], beside))
+        ys[-1].start()
+        to_sib(k + 1, block)
+    for k, d in enumerate((2, 1, 3)):
+        ys[k + 1].wait_recv()
+        to_sib(k + 4, ((z + 4 - d) % 4) * 2 + 1 - y)
+    for copy in ss + moves:
+        copy.wait_recv()
+    for copy in [core, cross, share] + moves + zs + ys + ss:
+        copy.wait_send()
+    stay.wait()
+    own.wait()
+
+
+def gather_tokens(part, hidden, gain, local, requests):
+    span, width = part.shape
+    half, quarter = width // 2, width // 4
+    context = local.shape[1]
+    vmem, anywhere = pl.BlockSpec(memory_space=pltpu.VMEM), pl.BlockSpec(memory_space=pl.ANY)
+    dma = pltpu.SemaphoreType.DMA
+    return pl.pallas_call(
+        gather_kernel,
+        out_shape=(
+            jax.ShapeDtypeStruct((requests, span, width), jnp.bfloat16),
+            jax.ShapeDtypeStruct((span, quarter), jnp.bfloat16),
+            jax.ShapeDtypeStruct((2, context // 4, width), jnp.bfloat16),
+        ),
+        in_specs=[vmem, vmem, vmem, anywhere],
+        out_specs=(anywhere, vmem, anywhere),
+        scratch_shapes=[pltpu.VMEM((span, half), jnp.bfloat16)] * 3
+        + [pltpu.VMEM((span, width), jnp.bfloat16)] * 2
+        + [dma((n,)) for n in (3, 3, 3, 3, 3, 3, 4, 4, 7, 7, 2)],
+        compiler_params=pltpu.CompilerParams(
+            collective_id=0, has_side_effects=True, vmem_limit_bytes=24 << 20
+        ),
+        name="gather_tokens",
+    )(part, hidden, gain, local)
+
+
+def return_kernel(
+    part, out, recv_a, send_x, recv_x, send_y, recv_y, send_z, recv_z, acc,
+    a_send, a_recv, x_send, x_recv, y_send, y_recv, z_send, z_recv,
+):
+    t, r, x, c, z, y = position()
+    _, span, width = part.shape
+    quarter = width // 4
+    sib = {"tensor": x * 2 + 1 - c}
+    across = {"tensor": (1 - x) * 2 + c}
+    beside = {"request": z * 2 + 1 - y}
+    line = [{"request": ((z + d) % 4) * 2 + y} for d in (1, 2, 3)]
+    meet([sib, across, beside] + line)
+
+    def columns(xx, cc):
+        return pl.ds(pl.multiple_of(quarter * (xx * 2 + cc), quarter), quarter)
+
+    blocks = [((z + d) % 4) * 2 + yy for yy in (1 - y, y) for d in (1, 2, 3, 4)]
+
+    def rows_of(step):
+        @pl.loop(0, span // ROWS)
+        def _(i):
+            step(pl.ds(pl.multiple_of(i * ROWS, ROWS), ROWS))
+
+    firsts, seconds = [], []
+    for k, block in enumerate(blocks):
+        for copies, j, xx in ((firsts, 0, 1 - x), (seconds, 1, x)):
+            copies.append(
+                remote(
+                    part.at[block, :, columns(xx, 1 - c)], recv_a.at[k, j],
+                    a_send.at[k, j], a_recv.at[k, j], sib,
+                )
+            )
+    for copy in firsts + seconds:
+        copy.start()
+    crossing = []
+    for k, block in enumerate(blocks):
+        firsts[k].wait_recv()
+
+        def outward(rows, k=k, block=block):
+            total = part[block, rows, columns(1 - x, c)].astype(jnp.float32) + recv_a[
+                k, 0, rows, :
+            ].astype(jnp.float32)
+            send_x[k, rows, :] = total.astype(jnp.bfloat16)
+
+        rows_of(outward)
+        crossing.append(
+            remote(send_x.at[k], recv_x.at[k], x_send.at[k], x_recv.at[k], across)
+        )
+        crossing[-1].start()
+    sides, ends = [], []
+    for k, block in enumerate(blocks):
+        seconds[k].wait_recv()
+        crossing[k].wait_recv()
+        if k >= 4:
+            sides[k - 4].wait_recv()
+
+        def inward(rows, k=k, block=block):
+            total = part[block, rows, columns(x, c)].astype(jnp.float32)
+            total = total + recv_a[k, 1, rows, :].astype(jnp.float32)
+            total = total + recv_x[k, rows, :].astype(jnp.float32)
+            if k < 4:
+                send_y[k, rows, :] = total.astype(jnp.bfloat16)
+                return
+            total = total + recv_y[k - 4, rows, :].astype(jnp.float32)
+            if k < 7:
+                send_z[k - 4, rows, :] = total.astype(jnp.bfloat16)
+            else:
+                acc[rows, :] = total
+
+        rows_of(inward)
+        if k < 4:
+            sides.append(remote(send_y.at[k], recv_y.at[k], y_send.at[k], y_recv.at[k], beside))
+            sides[-1].start()
+        elif k < 7:
+            i = k - 4
+            ends.append(remote(send_z.at[i], recv_z.at[i], z_send.at[i], z_recv.at[i], line[i]))
+            ends[-1].start()
+    for copy in ends:
+        copy.wait_recv()
+
+    def finish(rows):
+        total = acc[rows, :]
+        for i in range(3):
+            total = total + recv_z[i, rows, :].astype(jnp.float32)
+        out[rows, :] = total
+
+    rows_of(finish)
+    for copy in firsts + seconds + crossing + sides + ends:
+        copy.wait_send()
+
+
+def return_sums(part):
+    requests, span, width = part.shape
+    quarter = width // 4
+    vmem = pl.BlockSpec(memory_space=pltpu.VMEM)
+    dma = pltpu.SemaphoreType.DMA
+
+    def buffer(*lead):
+        return pltpu.VMEM((*lead, span, quarter), jnp.bfloat16)
+
+    return pl.pallas_call(
+        return_kernel,
+        out_shape=jax.ShapeDtypeStruct((span, quarter), jnp.float32),
+        in_specs=[vmem],
+        out_specs=vmem,
+        scratch_shapes=[
+            buffer(8, 2), buffer(8), buffer(8), buffer(4), buffer(4), buffer(3), buffer(3),
+            pltpu.VMEM((span, quarter), jnp.float32),
+            dma((8, 2)), dma((8, 2)), dma((8,)), dma((8,)), dma((4,)), dma((4,)), dma((3,)), dma((3,)),
+        ],
+        compiler_params=pltpu.CompilerParams(
+            collective_id=1, has_side_effects=True, vmem_limit_bytes=40 << 20
+        ),
+        name="return_sums",
+    )(part)
+
+
+def all_tokens(tokens, routes, route_weight, gate_w, up_w, down_w):
+    experts, span, width = tokens.shape
     ids = jnp.arange(experts, dtype=jnp.int32)
     spread = jnp.sum(
         jnp.where(routes[:, :, None] == ids, route_weight[:, :, None], 0.0), axis=1
     )
     weights = lax.all_to_all(spread, "request", split_axis=1, concat_axis=0, tiled=True)
-    tokens = lax.all_gather(normed, "request", axis=0, tiled=True)
+    tokens = tokens.reshape(experts * span, width)
     gate = jnp.dot(tokens, gate_w, preferred_element_type=jnp.float32)
     upper = jnp.dot(tokens, up_w, preferred_element_type=jnp.float32)
     act = (jax.nn.silu(gate) * upper * weights).astype(jnp.bfloat16)
     part = jnp.dot(act, down_w, preferred_element_type=jnp.float32).astype(jnp.bfloat16)
-    shares = lax.psum_scatter(part, "tensor", scatter_dimension=1, tiled=True)
-    total = lax.psum_scatter(shares, "request", scatter_dimension=0, tiled=True)
-    return total.astype(jnp.float32)
+    return return_sums(part.reshape(experts, span, width))
 
 
 def by_slots(normed, routes, route_weight, gate_w, up_w, down_w, experts, most):
@@ -107,6 +384,19 @@
     length = cached_len[0]
     attended = attend(span_q, span_k, span_v, cache_k, cache_v, length)
     attn_part = jnp.dot(attended, out_proj, preferred_element_type=jnp.float32)
+    context = cache_k.shape[1] + span
+    local = jnp.stack(
+        [place(cache_k, span_k, length, context), place(cache_v, span_v, length, context)], axis=0
+    )
+    experts = lax.axis_size("request")
+    most = max(2, 2 * span * TOP // experts)
+    if groups == 4 and experts == 8 and most >= span:
+        tokens, own_mixed, decode_kv = gather_tokens(
+            attn_part.astype(jnp.bfloat16), hidden_in, norm_gain[None, :], local, experts
+        )
+        mixture = all_tokens(tokens, routes, route_weight, w_gate[0], w_up[0], w_down[0])
+        layer_out = (own_mixed.astype(jnp.float32) + mixture).astype(jnp.bfloat16)
+        return (layer_out, decode_kv[None])
     attn_full = lax.psum(attn_part.astype(jnp.bfloat16), "tensor").astype(jnp.float32)
     mixed = (hidden_in.astype(jnp.float32) + attn_full).astype(jnp.bfloat16)
     mixed_f = mixed.astype(jnp.float32)
@@ -114,20 +404,11 @@
         mixed_f * lax.rsqrt(jnp.mean(mixed_f * mixed_f, axis=1, keepdims=True) + eps) * norm_gain
     ).astype(jnp.bfloat16)
     own_mixed = lax.dynamic_slice_in_dim(mixed, offset, quarter, 1)
-    experts = lax.axis_size("request")
-    most = max(2, 2 * span * TOP // experts)
-    if most >= span:
-        mixture = all_tokens(normed, routes, route_weight, w_gate[0], w_up[0], w_down[0], experts)
-    else:
-        mixture = by_slots(
-            normed, routes, route_weight, w_gate[0], w_up[0], w_down[0], experts, most
-        )
+    mixture = by_slots(
+        normed, routes, route_weight, w_gate[0], w_up[0], w_down[0], experts, most
+    )
     layer_out = (own_mixed.astype(jnp.float32) + mixture).astype(jnp.bfloat16)
-    context = cache_k.shape[1] + span
-    local = jnp.stack(
-        [place(cache_k, span_k, length, context), place(cache_v, span_v, length, context)], axis=0
-    )[None]
-    decode_kv = lax.all_to_all(local, "tensor", split_axis=2, concat_axis=3, tiled=True)
+    decode_kv = lax.all_to_all(local[None], "tensor", split_axis=2, concat_axis=3, tiled=True)
     return (layer_out, decode_kv)
 
 

time: 365 us -> 208 us (0.57)
  waiting for transfers between devices: 272 us -> 0.01 us
  Pallas kernels: 0 us -> 152 us
  between operations: 14.8 us -> 1.53 us
  local copies, waits for them, and re-layouts: 27.1 us -> 16.8 us
  matrix products: 27.6 us -> 20.1 us
    pallas_call x0 -> x2, Pallas kernels: none -> 152 us  [the longest x1 93.8 us: gather_tokens(): pl.pallas_call(gather_kernel, out_shape=(jax.ShapeDtypeStruct((requests,...]
    all_gather x1 -> x0, waiting for transfers between devices: 119 us -> none  [all_tokens(): tokens = lax.all_gather(normed, 'request', axis=0, tiled=True)]
    reduce_scatter x2 -> x0, waiting for transfers between devices: 88.2 us -> none  [the longest x1 70 us: all_tokens(): shares = lax.psum_scatter(part, 'tensor', scatter_dimension=1, tiled=True)]
    psum x1 -> x0, waiting for transfers between devices: 38.9 us -> none  [on_device(): lax.psum(attn_part.astype(jnp.bfloat16), 'tensor').astype(jnp.float32)]
    all_to_all x1 -> x0, waiting for transfers between devices: 25.8 us -> none  [on_device(): lax.all_to_all(local, 'tensor', split_axis=2, concat_axis=3, tiled=True)]
    all_to_all x2 -> x0, local copies, waits for them, and re-layouts: 9 us -> none  [on_device(): lax.all_to_all(local, 'tensor', split_axis=2, concat_axis=3, tiled=True)]
    all_to_all x1 -> x0, starting transfers between devices: 4.45 us -> none  [on_device(): lax.all_to_all(local, 'tensor', split_axis=2, concat_axis=3, tiled=True)]
    unnamed x24 -> x35, local copies, waits for them, and re-layouts: 5.43 us -> 8.69 us
  transfers between devices with their start and end apart: 6 -> 1, of which waited for: 5 -> 0; matrix products, arithmetic and copies ran while one was open for 8% -> 14% of each run, Pallas kernels for 0% -> 45%
where the time goes in v2:
time: 208 us
  Pallas kernels  152 us (73%)
  matrix products  20.1 us (10%)
  local copies, waits for them, and re-layouts  16.8 us (8%)
  other arithmetic  9.47 us (5%)
  starting transfers between devices  7.28 us (4%)
    pallas_call x1, Pallas kernels, gather_tokens(): pl.pallas_call(gather_kernel, out_shape=(jax.ShapeDtypeStruct((requests,...  93.8 us
    pallas_call x1, Pallas kernels, return_sums(): pl.pallas_call(return_kernel, out_shape=jax.ShapeDtypeStruct((span, quart...  58.6 us
    unnamed x35, local copies, waits for them, and re-layouts  8.69 us
    dot_general x1, matrix products, all_tokens(): upper = jnp.dot(tokens, up_w, preferred_element_type=jnp.float32)  8.12 us
    all_to_all x1, starting transfers between devices, all_tokens(): lax.all_to_all(spread, 'request', split_axis=1, concat_axis=0, tiled=True)  7.28 us
    dynamic_update_slice x2, local copies, waits for them, and re-layouts, place(): return lax.dynamic_update_slice(kept, fresh, (length, jnp.int32(0)))  5.48 us
    dot_general x1, matrix products, all_tokens(): gate = jnp.dot(tokens, gate_w, preferred_element_type=jnp.float32)  5.08 us
    dot_general x1, matrix products, all_tokens(): jnp.dot(act, down_w, preferred_element_type=jnp.float32)  4.97 us
  transfers between devices with their start and end apart: 1, of which 0 were waited for; matrix products, arithmetic and copies ran while one was open for 14% of the time, Pallas kernels for 45%

profile of v2, /device:TPU:0, one launch (start us, length us, event | category | flops | bytes accessed | tf_op | source)
XLA Modules:
  0.0 207.6 jit_solution(13837832945831822838)
XLA Ops:
  0.6 0.9 select_reduce_fusion
  1.5 0.6 copy.50
  2.1 7.3 %all-to-all-start = ((f32[256,8,1]{0,2,1:T(1,128)}), f32[256,8,1]{0,2,1:T(1,128)S(1)}, u32[]{:S(2)}, u32[]{:S(2)}) async-start(f32[256,8,1]{0,2,1:T(1,128)} %copy.50), calls=%async_computation | async-start | bytes 16384 | tf_op jit(solution)/shard_map/all_to_all | solution.py:327
  10.1 1.1 copy.45
  11.2 0.8 copy.47
  12.0 1.8 copy.43
  13.8 1.4 copy.44
  15.2 1.2 copy.46
  16.4 2.3 %copy.42 = bf16[1,768,512]{1,2,0:T(8,128)(2,1)} copy(bf16[1,768,512]{2,1,0:T(8,128)(2,1)} %param.19) | data formatting | bytes 1572864 | tf_op args[5]
  18.7 1.5 fusion.20
  20.2 2.7 %select_bitcast_fusion.1 = (bf16[1,1024,512]{2,1,0:T(8,128)(2,1)}, bf16[1,1024,512]{2,1,0:T(8,128)(2,1)S(1)}) fusion(bf16[768,512]{1,0:T(8,128)(2,1)} %bitcast.66, pred[1024]{0:T(1024)(128)(4,1)S(1)} %get-tuple-element.12, bf16[768,512]{1,0:T(8,128)(2,1)} %bitcast.67), kind=kLoop, calls=%fused_computation.28 | loop fusion | flops 1048576 | bytes 3671040 | tf_op jit(solution)/shard_map/stack | solution.py:388
  22.9 2.8 %dynamic_update_slice.8 = bf16[1,1024,512]{2,1,0:T(8,128)(2,1)} dynamic-update-slice(bf16[1,1024,512]{2,1,0:T(8,128)(2,1)} %get-tuple-element.8, bf16[1,256,512]{2,1,0:T(8,128)(2,1)S(1)} %bitcast.68, s32[]{:T(128)} %constant.21.clone.1, s32[]{:T(128)S(6)} %select_n.30, s32[]{:T(128)} %constant.21.clone.1) | dynamic-update-slice | bytes 524292 | tf_op jit(solution)/shard_map/dynamic_update_slice | solution.py:42
  25.7 2.7 %dynamic_update_slice.9 = bf16[1,1024,512]{2,1,0:T(8,128)(2,1)S(1)} dynamic-update-slice(bf16[1,1024,512]{2,1,0:T(8,128)(2,1)S(1)} %get-tuple-element.9, bf16[1,256,512]{2,1,0:T(8,128)(2,1)} %bitcast.69, s32[]{:T(128)} %constant.21.clone.1, s32[]{:T(128)S(6)} %select_n.30, s32[]{:T(128)} %constant.21.clone.1) | dynamic-update-slice | bytes 524292 | tf_op jit(solution)/shard_map/dynamic_update_slice | solution.py:42
  28.4 1.5 pad_maximum_fusion.local
  30.0 0.7 fusion.16
  30.9 2.1 %fusion.27 = (f32[4,256]{1,0:T(4,128)S(1)}, f32[4,256,1024]{1,2,0:T(8,128)S(1)}) fusion(f32[4,1024,256]{2,1,0:T(8,128)S(1)} %fusion.16, pred[256,1024]{0,1:T(8,128)(4,1)S(1)} %copy-done.11), kind=kOutput, calls=%fused_computation.43 | output fusion | flops 6292479 | bytes 8654848 | tf_op jit(solution)/shard_map/sub | solution.py:31
  33.6 0.7 convolution_convert_fusion.1.part
  34.8 93.8 %gather_tokens.1 = (bf16[8,256,2048]{2,1,0:T(8,128)(2,1)S(1)}, bf16[256,512]{1,0:T(8,128)(2,1)S(1)}, bf16[2,256,2048]{2,1,0:T(8,128)(2,1)S(1)}) custom-call(bf16[256,2048]{1,0:T(8,128)(2,1)S(1)} %convolution_convert_fusion.1.part, bf16[256,2048]{1,0:T(8,128)(2,1)S(1)} %copy-done.3, f32[1,2048]{1,0:T(1,128)S(1)} %bitcast.62, ...), custom_call_target="tpu_custom_call" | custom-call | tf_op jit(solution)/shard_map/gather_tokens/pallas_call | solution.py:185
  128.7 5.1 %fusion.10 = f32[2048,352]{0,1:T(8,128)} fusion(bf16[2048,2048]{1,0:T(8,128)(2,1)S(1)} %bitcast.63, bf16[1,2048,352]{1,2,0:T(8,128)(2,1)S(1)} %copy-done.13), kind=kOutput, calls=%fused_computation.17 | convolution fusion | flops 2952790016 | bytes 12713984 | tf_op jit(solution)/shard_map/dot_general | solution.py:329
  133.8 8.1 %fusion.3 = bf16[2048,352]{0,1:T(8,128)(2,1)S(1)} fusion(bf16[2048,2048]{1,0:T(8,128)(2,1)} %bitcast.64, f32[2048,352]{0,1:T(8,128)} %fusion.10, bf16[1,2048,352]{1,2,0:T(8,128)(2,1)} %param.26, f32[2048]{0:T(1024)S(1)} %bitcast.75), kind=kOutput, calls=%fused_computation.8 | convolution fusion | flops 2957836288 | bytes 14163968 | tf_op jit(solution)/shard_map/dot_general | solution.py:330
  141.9 5.0 %convolution_convert_fusion = bf16[2048,2048]{1,0:T(8,128)(2,1)S(1)} fusion(bf16[2048,352]{0,1:T(8,128)(2,1)S(1)} %fusion.3, bf16[1,352,2048]{2,1,0:T(8,128)(2,1)S(1)} %copy-done.14), kind=kOutput, calls=%fused_computation.1 | convolution fusion | flops 2956984320 | bytes 11272192 | tf_op jit(solution)/shard_map/dot_general | solution.py:332
  146.9 58.6 %return_sums.1 = f32[256,512]{1,0:T(8,128)S(1)} custom-call(bf16[8,256,2048]{2,1,0:T(8,128)(2,1)S(1)} %bitcast.60), custom_call_target="tpu_custom_call" | custom-call | tf_op jit(solution)/shard_map/return_sums/pallas_call | solution.py:304
  205.5 0.8 add_convert_fusion
  206.3 1.3 copy.61
  (34 shorter events, 1.2 us)
Async XLA Ops:
  0.6 33.0 %copy-start = (bf16[512,2048]{1,0:T(8,128)(2,1)S(1)}, bf16[512,2048]{1,0:T(8,128)(2,1)}, u32[]{:S(2)}) copy-start(bf16[512,2048]{1,0:T(8,128)(2,1)} %param.21) | copy-start | bytes 6291460
  2.1 131.6 %all-to-all-start = ((f32[256,8,1]{0,2,1:T(1,128)}), f32[256,8,1]{0,2,1:T(1,128)S(1)}, u32[]{:S(2)}, u32[]{:S(2)}) async-start(f32[256,8,1]{0,2,1:T(1,128)} %copy.50), calls=%async_computation | async-start | bytes 16384 | tf_op jit(solution)/shard_map/all_to_all | solution.py:327
  16.4 6.5 %copy-start.7 = (bf16[256,512]{1,0:T(8,128)(2,1)S(1)}, bf16[256,512]{1,0:T(8,128)(2,1)}, u32[]{:S(2)}) copy-start(bf16[256,512]{1,0:T(8,128)(2,1)} %param.16) | copy-start | bytes 786436
  25.7 4.2 %copy-start.8 = (bf16[256,4,128]{2,0,1:T(8,128)(2,1)S(1)}, bf16[256,4,128]{2,0,1:T(8,128)(2,1)}, u32[]{:S(2)}) copy-start(bf16[256,4,128]{2,0,1:T(8,128)(2,1)} %copy.47) | copy-start | bytes 786436
  28.4 1.5 copy-start.6
  28.4 1.5 copy-start.12
  30.0 1.0 copy-start.11
  30.9 2.1 %copy-start.9 = (bf16[1,768,512]{1,2,0:T(8,128)(2,1)S(1)}, bf16[1,768,512]{1,2,0:T(8,128)(2,1)}, u32[]{:S(2)}) copy-start(bf16[1,768,512]{1,2,0:T(8,128)(2,1)} %copy.42) | copy-start | bytes 2359300
  30.9 2.1 %copy-start.10 = (bf16[256,512]{0,1:T(8,128)(2,1)S(1)}, bf16[256,512]{0,1:T(8,128)(2,1)}, u32[]{:S(2)}) copy-start(bf16[256,512]{0,1:T(8,128)(2,1)} %copy.43) | copy-start | bytes 786436
  33.6 1.2 copy-start.3
  33.6 1.2 copy-start.4
  34.3 94.3 %copy-start.13 = (bf16[1,2048,352]{1,2,0:T(8,128)(2,1)S(1)}, bf16[1,2048,352]{1,2,0:T(8,128)(2,1)}, u32[]{:S(2)}) copy-start(bf16[1,2048,352]{1,2,0:T(8,128)(2,1)} %param.25) | copy-start | bytes 4325380
  128.6 5.1 %copy-start.1 = (bf16[2,256,2048]{2,1,0:T(8,128)(2,1)}, bf16[2,256,2048]{2,1,0:T(8,128)(2,1)S(1)}, u32[]{:S(2)}) copy-start(bf16[2,256,2048]{2,1,0:T(8,128)(2,1)S(1)} %get-tuple-element.7) | copy-start | bytes 6291460
  128.6 5.1 %copy-start.5 = (bf16[8,256,2048]{2,1,0:T(8,128)(2,1)}, bf16[8,256,2048]{2,1,0:T(8,128)(2,1)S(1)}, u32[]{:S(2)}) copy-start(bf16[8,256,2048]{2,1,0:T(8,128)(2,1)S(1)} %get-tuple-element.6) | copy-start | bytes 25165828
  133.7 8.1 %copy-start.14 = (bf16[1,352,2048]{2,1,0:T(8,128)(2,1)S(1)}, bf16[1,352,2048]{2,1,0:T(8,128)(2,1)}, u32[]{:S(2)}) copy-start(bf16[1,352,2048]{2,1,0:T(8,128)(2,1)} %param.27) | copy-start | bytes 4325380
  146.9 59.4 %copy-start.2 = (bf16[2,256,2048]{2,1,0:T(8,128)(2,1)S(1)}, bf16[2,256,2048]{2,1,0:T(8,128)(2,1)}, u32[]{:S(2)}) copy-start(bf16[2,256,2048]{2,1,0:T(8,128)(2,1)} %copy-done.1) | copy-start | bytes 6291460

commit v3 on v2

--- a/solution.py
+++ b/solution.py
@@ -44,6 +44,7 @@
 
 MESH = pl.DeviceIdType.MESH
 ROWS = 64
+PIECES = 2
 
 
 def remote(src, dst, send, recv, device):
@@ -138,36 +139,37 @@
     own = pltpu.make_async_copy(normed, tokens.at[r], own_sem.at[1])
     own.start()
     zs, ys, ss = [], [], []
-    for d in (2, 1, 3):
-        zs.append(
-            remote(
-                normed.at[:, mine], tokens.at[r, :, mine], z_send.at[d - 1], z_recv.at[d - 1],
-                line[d - 1],
+    piece = span // PIECES
+    bits = [pl.ds(q * piece, piece) for q in range(PIECES)]
+    for q, rows in enumerate(bits):
+        src, dst = normed.at[rows, mine], tokens.at[r, rows, mine]
+        ys.append(remote(src, dst, y_send.at[q, 0], y_recv.at[q, 0], beside))
+        ys[-1].start()
+        for d in (2, 1, 3):
+            zs.append(remote(src, dst, z_send.at[q, d - 1], z_recv.at[q, d - 1], line[d - 1]))
+            zs[-1].start()
+
+    def to_sib(q, k, block):
+        view = tokens.at[block, bits[q], mine]
+        ss.append(remote(view, view, s_send.at[q, k], s_recv.at[q, k], sib))
+        ss[-1].start()
+
+    for q, rows in enumerate(bits):
+        ys[q].wait_recv()
+        to_sib(q, 0, z * 2 + 1 - y)
+        for k, d in enumerate((2, 1, 3)):
+            zs[3 * q + k].wait_recv()
+            block = ((z + 4 - d) % 4) * 2 + y
+            view = tokens.at[block, rows, mine]
+            ys.append(
+                remote(view, view, y_send.at[q, k + 1], y_recv.at[q, k + 1], beside)
             )
-        )
-    ys.append(
-        remote(normed.at[:, mine], tokens.at[r, :, mine], y_send.at[0], y_recv.at[0], beside)
-    )
-    for copy in ys + zs:
-        copy.start()
-
-    def to_sib(k, block):
-        view = tokens.at[block, :, mine]
-        ss.append(remote(view, view, s_send.at[k], s_recv.at[k], sib))
-        ss[-1].start()
-
-    ys[0].wait_recv()
-    to_sib(0, z * 2 + 1 - y)
-    for k, d in enumerate((2, 1, 3)):
-        zs[k].wait_recv()
-        block = ((z + 4 - d) % 4) * 2 + y
-        view = tokens.at[block, :, mine]
-        ys.append(remote(view, view, y_send.at[k + 1], y_recv.at[k + 1], beside))
-        ys[-1].start()
-        to_sib(k + 1, block)
-    for k, d in enumerate((2, 1, 3)):
-        ys[k + 1].wait_recv()
-        to_sib(k + 4, ((z + 4 - d) % 4) * 2 + 1 - y)
+            ys[-1].start()
+            to_sib(q, k + 1, block)
+    for q in range(PIECES):
+        for k, d in enumerate((2, 1, 3)):
+            ys[PIECES + 3 * q + k].wait_recv()
+            to_sib(q, k + 4, ((z + 4 - d) % 4) * 2 + 1 - y)
     for copy in ss + moves:
         copy.wait_recv()
     for copy in [core, cross, share] + moves + zs + ys + ss:
@@ -193,7 +195,9 @@
         out_specs=(anywhere, vmem, anywhere),
         scratch_shapes=[pltpu.VMEM((span, half), jnp.bfloat16)] * 3
         + [pltpu.VMEM((span, width), jnp.bfloat16)] * 2
-        + [dma((n,)) for n in (3, 3, 3, 3, 3, 3, 4, 4, 7, 7, 2)],
+        + [dma((n,)) for n in (3, 3, 3, 3)]
+        + [dma((PIECES, n)) for n in (3, 3, 4, 4, 7, 7)]
+        + [dma((2,))],
         compiler_params=pltpu.CompilerParams(
             collective_id=0, has_side_effects=True, vmem_limit_bytes=24 << 20
         ),

time: 208 us -> 197 us (0.947)
  Pallas kernels: 152 us -> 141 us
    pallas_call x1, Pallas kernels: 93.8 us -> 81.8 us  [gather_tokens(): pl.pallas_call(gather_kernel, out_shape=(jax.ShapeDtypeStruct((requests,...]
  transfers between devices with their start and end apart: 1 -> 1, of which waited for: 0 -> 0; matrix products, arithmetic and copies ran while one was open for 14% -> 15% of each run, Pallas kernels for 45% -> 42%
where the time goes in v3:
time: 197 us; the launch traced here: 196 us
  Pallas kernels  141 us (72%)
  matrix products  20.1 us (10%)
  local copies, waits for them, and re-layouts  16.8 us (9%)
  other arithmetic  9.47 us (5%)
  starting transfers between devices  7.28 us (4%)
    pallas_call x1, Pallas kernels, gather_tokens(): pl.pallas_call(gather_kernel, out_shape=(jax.ShapeDtypeStruct((requests,...  81.8 us
    pallas_call x1, Pallas kernels, return_sums(): pl.pallas_call(return_kernel, out_shape=jax.ShapeDtypeStruct((span, quart...  59.4 us
    unnamed x35, local copies, waits for them, and re-layouts  8.69 us
    dot_general x1, matrix products, all_tokens(): upper = jnp.dot(tokens, up_w, preferred_element_type=jnp.float32)  8.11 us
    all_to_all x1, starting transfers between devices, all_tokens(): lax.all_to_all(spread, 'request', split_axis=1, concat_axis=0, tiled=True)  7.28 us
    dynamic_update_slice x2, local copies, waits for them, and re-layouts, place(): return lax.dynamic_update_slice(kept, fresh, (length, jnp.int32(0)))  5.48 us
    dot_general x1, matrix products, all_tokens(): gate = jnp.dot(tokens, gate_w, preferred_element_type=jnp.float32)  5.08 us
    dot_general x1, matrix products, all_tokens(): jnp.dot(act, down_w, preferred_element_type=jnp.float32)  4.97 us
  transfers between devices with their start and end apart: 1, of which 0 were waited for; matrix products, arithmetic and copies ran while one was open for 15% of the time, Pallas kernels for 42%

profile of v3, /device:TPU:0, one launch (start us, length us, event | category | flops | bytes accessed | tf_op | source)
XLA Modules:
  0.0 196.4 jit_solution(4495658782429451081)
XLA Ops:
  0.6 0.9 select_reduce_fusion
  1.5 0.6 copy.50
  2.1 7.3 %all-to-all-start = ((f32[256,8,1]{0,2,1:T(1,128)}), f32[256,8,1]{0,2,1:T(1,128)S(1)}, u32[]{:S(2)}, u32[]{:S(2)}) async-start(f32[256,8,1]{0,2,1:T(1,128)} %copy.50), calls=%async_computation | async-start | bytes 16384 | tf_op jit(solution)/shard_map/all_to_all | solution.py:331
  10.1 1.1 copy.45
  11.2 0.8 copy.47
  12.0 1.8 copy.43
  13.8 1.4 copy.44
  15.2 1.2 copy.46
  16.4 2.3 %copy.42 = bf16[1,768,512]{1,2,0:T(8,128)(2,1)} copy(bf16[1,768,512]{2,1,0:T(8,128)(2,1)} %param.19) | data formatting | bytes 1572864 | tf_op args[5]
  18.7 1.5 fusion.20
  20.2 2.7 %select_bitcast_fusion.1 = (bf16[1,1024,512]{2,1,0:T(8,128)(2,1)}, bf16[1,1024,512]{2,1,0:T(8,128)(2,1)S(1)}) fusion(bf16[768,512]{1,0:T(8,128)(2,1)} %bitcast.66, pred[1024]{0:T(1024)(128)(4,1)S(1)} %get-tuple-element.12, bf16[768,512]{1,0:T(8,128)(2,1)} %bitcast.67), kind=kLoop, calls=%fused_computation.28 | loop fusion | flops 1048576 | bytes 3671040 | tf_op jit(solution)/shard_map/stack | solution.py:392
  22.9 2.8 %dynamic_update_slice.8 = bf16[1,1024,512]{2,1,0:T(8,128)(2,1)} dynamic-update-slice(bf16[1,1024,512]{2,1,0:T(8,128)(2,1)} %get-tuple-element.8, bf16[1,256,512]{2,1,0:T(8,128)(2,1)S(1)} %bitcast.68, s32[]{:T(128)} %constant.21.clone.1, s32[]{:T(128)S(6)} %select_n.30, s32[]{:T(128)} %constant.21.clone.1) | dynamic-update-slice | bytes 524292 | tf_op jit(solution)/shard_map/dynamic_update_slice | solution.py:42
  25.7 2.7 %dynamic_update_slice.9 = bf16[1,1024,512]{2,1,0:T(8,128)(2,1)S(1)} dynamic-update-slice(bf16[1,1024,512]{2,1,0:T(8,128)(2,1)S(1)} %get-tuple-element.9, bf16[1,256,512]{2,1,0:T(8,128)(2,1)} %bitcast.69, s32[]{:T(128)} %constant.21.clone.1, s32[]{:T(128)S(6)} %select_n.30, s32[]{:T(128)} %constant.21.clone.1) | dynamic-update-slice | bytes 524292 | tf_op jit(solution)/shard_map/dynamic_update_slice | solution.py:42
  28.4 1.5 pad_maximum_fusion.local
  30.0 0.7 fusion.16
  30.9 2.1 %fusion.27 = (f32[4,256]{1,0:T(4,128)S(1)}, f32[4,256,1024]{1,2,0:T(8,128)S(1)}) fusion(f32[4,1024,256]{2,1,0:T(8,128)S(1)} %fusion.16, pred[256,1024]{0,1:T(8,128)(4,1)S(1)} %copy-done.11), kind=kOutput, calls=%fused_computation.43 | output fusion | flops 6292479 | bytes 8654848 | tf_op jit(solution)/shard_map/sub | solution.py:31
  33.6 0.7 convolution_convert_fusion.1.part
  34.8 81.8 %gather_tokens.1 = (bf16[8,256,2048]{2,1,0:T(8,128)(2,1)S(1)}, bf16[256,512]{1,0:T(8,128)(2,1)S(1)}, bf16[2,256,2048]{2,1,0:T(8,128)(2,1)S(1)}) custom-call(bf16[256,2048]{1,0:T(8,128)(2,1)S(1)} %convolution_convert_fusion.1.part, bf16[256,2048]{1,0:T(8,128)(2,1)S(1)} %copy-done.3, f32[1,2048]{1,0:T(1,128)S(1)} %bitcast.62, ...), custom_call_target="tpu_custom_call" | custom-call | tf_op jit(solution)/shard_map/gather_tokens/pallas_call | solution.py:187
  116.7 5.1 %fusion.10 = f32[2048,352]{0,1:T(8,128)} fusion(bf16[2048,2048]{1,0:T(8,128)(2,1)S(1)} %bitcast.63, bf16[1,2048,352]{1,2,0:T(8,128)(2,1)S(1)} %copy-done.13), kind=kOutput, calls=%fused_computation.17 | convolution fusion | flops 2952790016 | bytes 12713984 | tf_op jit(solution)/shard_map/dot_general | solution.py:333
  121.8 8.1 %fusion.3 = bf16[2048,352]{0,1:T(8,128)(2,1)S(1)} fusion(bf16[2048,2048]{1,0:T(8,128)(2,1)} %bitcast.64, f32[2048,352]{0,1:T(8,128)} %fusion.10, bf16[1,2048,352]{1,2,0:T(8,128)(2,1)} %param.26, f32[2048]{0:T(1024)S(1)} %bitcast.75), kind=kOutput, calls=%fused_computation.8 | convolution fusion | flops 2957836288 | bytes 14163968 | tf_op jit(solution)/shard_map/dot_general | solution.py:334
  129.9 5.0 %convolution_convert_fusion = bf16[2048,2048]{1,0:T(8,128)(2,1)S(1)} fusion(bf16[2048,352]{0,1:T(8,128)(2,1)S(1)} %fusion.3, bf16[1,352,2048]{2,1,0:T(8,128)(2,1)S(1)} %copy-done.14), kind=kOutput, calls=%fused_computation.1 | convolution fusion | flops 2956984320 | bytes 11272192 | tf_op jit(solution)/shard_map/dot_general | solution.py:336
  134.9 59.4 %return_sums.1 = f32[256,512]{1,0:T(8,128)S(1)} custom-call(bf16[8,256,2048]{2,1,0:T(8,128)(2,1)S(1)} %bitcast.60), custom_call_target="tpu_custom_call" | custom-call | tf_op jit(solution)/shard_map/return_sums/pallas_call | solution.py:308
  194.3 0.8 add_convert_fusion
  195.1 1.3 copy.61
  (34 shorter events, 1.2 us)
Async XLA Ops:
  0.6 33.0 %copy-start = (bf16[512,2048]{1,0:T(8,128)(2,1)S(1)}, bf16[512,2048]{1,0:T(8,128)(2,1)}, u32[]{:S(2)}) copy-start(bf16[512,2048]{1,0:T(8,128)(2,1)} %param.21) | copy-start | bytes 6291460
  2.1 119.6 %all-to-all-start = ((f32[256,8,1]{0,2,1:T(1,128)}), f32[256,8,1]{0,2,1:T(1,128)S(1)}, u32[]{:S(2)}, u32[]{:S(2)}) async-start(f32[256,8,1]{0,2,1:T(1,128)} %copy.50), calls=%async_computation | async-start | bytes 16384 | tf_op jit(solution)/shard_map/all_to_all | solution.py:331
  16.4 6.5 %copy-start.7 = (bf16[256,512]{1,0:T(8,128)(2,1)S(1)}, bf16[256,512]{1,0:T(8,128)(2,1)}, u32[]{:S(2)}) copy-start(bf16[256,512]{1,0:T(8,128)(2,1)} %param.16) | copy-start | bytes 786436
  25.7 4.2 %copy-start.8 = (bf16[256,4,128]{2,0,1:T(8,128)(2,1)S(1)}, bf16[256,4,128]{2,0,1:T(8,128)(2,1)}, u32[]{:S(2)}) copy-start(bf16[256,4,128]{2,0,1:T(8,128)(2,1)} %copy.47) | copy-start | bytes 786436
  28.4 1.5 copy-start.6
  28.4 1.5 copy-start.12
  30.0 1.0 copy-start.11
  30.9 2.1 %copy-start.9 = (bf16[1,768,512]{1,2,0:T(8,128)(2,1)S(1)}, bf16[1,768,512]{1,2,0:T(8,128)(2,1)}, u32[]{:S(2)}) copy-start(bf16[1,768,512]{1,2,0:T(8,128)(2,1)} %copy.42) | copy-start | bytes 2359300
  30.9 2.1 %copy-start.10 = (bf16[256,512]{0,1:T(8,128)(2,1)S(1)}, bf16[256,512]{0,1:T(8,128)(2,1)}, u32[]{:S(2)}) copy-start(bf16[256,512]{0,1:T(8,128)(2,1)} %copy.43) | copy-start | bytes 786436
  33.6 1.2 copy-start.3
  33.6 1.2 copy-start.4
  34.3 82.3 %copy-start.13 = (bf16[1,2048,352]{1,2,0:T(8,128)(2,1)S(1)}, bf16[1,2048,352]{1,2,0:T(8,128)(2,1)}, u32[]{:S(2)}) copy-start(bf16[1,2048,352]{1,2,0:T(8,128)(2,1)} %param.25) | copy-start | bytes 4325380
  116.6 5.1 %copy-start.1 = (bf16[2,256,2048]{2,1,0:T(8,128)(2,1)}, bf16[2,256,2048]{2,1,0:T(8,128)(2,1)S(1)}, u32[]{:S(2)}) copy-start(bf16[2,256,2048]{2,1,0:T(8,128)(2,1)S(1)} %get-tuple-element.7) | copy-start | bytes 6291460
  116.6 5.1 %copy-start.5 = (bf16[8,256,2048]{2,1,0:T(8,128)(2,1)}, bf16[8,256,2048]{2,1,0:T(8,128)(2,1)S(1)}, u32[]{:S(2)}) copy-start(bf16[8,256,2048]{2,1,0:T(8,128)(2,1)S(1)} %get-tuple-element.6) | copy-start | bytes 25165828
  121.7 8.1 %copy-start.14 = (bf16[1,352,2048]{2,1,0:T(8,128)(2,1)S(1)}, bf16[1,352,2048]{2,1,0:T(8,128)(2,1)}, u32[]{:S(2)}) copy-start(bf16[1,352,2048]{2,1,0:T(8,128)(2,1)} %param.27) | copy-start | bytes 4325380
  134.9 60.2 %copy-start.2 = (bf16[2,256,2048]{2,1,0:T(8,128)(2,1)S(1)}, bf16[2,256,2048]{2,1,0:T(8,128)(2,1)}, u32[]{:S(2)}) copy-start(bf16[2,256,2048]{2,1,0:T(8,128)(2,1)} %copy-done.1) | copy-start | bytes 6291460
